TPU v7x, 32 devices: a whole 2x2x4 slice. The times are simulated.
32 devices in a mesh: dp: 4 (over y, core), fsdp: 4 (over z), seq: 2 (over x).
Axes of the slice: x: 2, y: 2, z: 4, core: 2. Of those that a mesh axis runs over, the one named last changes fastest.
Arguments:
- queries: bfloat16 [16, 256, 2048], P(('dp', 'fsdp'), 'seq'), may hold values from -30 to 30
- key_rows: bfloat16 [16, 256, 2048], P(('dp', 'fsdp'), 'seq'), may hold values from -12 to 12
- value_rows: bfloat16 [16, 256, 2048], P(('dp', 'fsdp'), 'seq'), may hold values from -6 to 6
- cotangent: bfloat16 [16, 256, 2048], P(('dp', 'fsdp'), 'seq'), may hold values from -6 to 6
- out_weight: bfloat16 [2048, 2048], P('fsdp'), may hold values from -0.125 to 0.125
Outputs:
- query_grad: bfloat16 [16, 256, 2048], P(('dp', 'fsdp'), 'seq')
- key_grad: bfloat16 [16, 256, 2048], P(('dp', 'fsdp'), 'seq')
- value_grad: bfloat16 [16, 256, 2048], P(('dp', 'fsdp'), 'seq')
- weight_grad: float32 [2048, 2048], P('fsdp')
All inputs are finite; a program needn't handle non-finite values.
Results may differ from a plain program's by a relative error of at most 0.014.
Values may be sent and summed in bfloat16 or wider, within the bound.
A program may use at most 128 MiB of HBM per device.

v0:
```python
import jax
import jax.numpy as jnp
from jax import lax
from jax.sharding import PartitionSpec as P

DH = 128


def head_backward(query_head, key_head, value_head, grad_head, block_rows):
    length = key_head.shape[0]
    score_scale = DH ** (-0.5)
    blocks = length // block_rows

    def visit(carry, block):
        key_acc, value_acc = carry
        begin = block * block_rows
        query_block = lax.dynamic_slice_in_dim(query_head, begin, block_rows, 0)
        grad_block = lax.dynamic_slice_in_dim(grad_head, begin, block_rows, 0)
        scores = (
            jnp.einsum("qd,kd->qk", query_block, key_head, preferred_element_type=jnp.float32)
            * score_scale
        )
        highest = jnp.max(scores, axis=1, keepdims=True)
        expanded = jnp.exp(scores - highest)
        weights = expanded / jnp.sum(expanded, axis=1, keepdims=True)
        weights_half = weights.astype(jnp.bfloat16)
        attended = jnp.einsum(
            "qk,kd->qd", weights_half, value_head, preferred_element_type=jnp.float32
        ).astype(jnp.bfloat16)
        grad_weights = jnp.einsum(
            "qd,kd->qk", grad_block, value_head, preferred_element_type=jnp.float32
        )
        row_delta = jnp.sum(weights * grad_weights, axis=1, keepdims=True)
        grad_scores = (weights * (grad_weights - row_delta)).astype(jnp.bfloat16)
        query_grad = (
            jnp.einsum("qk,kd->qd", grad_scores, key_head, preferred_element_type=jnp.float32)
            * score_scale
        ).astype(jnp.bfloat16)
        key_acc = key_acc + jnp.einsum(
            "qk,qd->kd", grad_scores, query_block, preferred_element_type=jnp.float32
        )
        value_acc = value_acc + jnp.einsum(
            "qk,qd->kd", weights_half, grad_block, preferred_element_type=jnp.float32
        )
        return ((key_acc, value_acc), (attended, query_grad))

    empty = jnp.zeros(key_head.shape, jnp.float32)
    finals, stacked = lax.scan(visit, (empty, empty), jnp.arange(blocks))
    attended = stacked[0].reshape(length, DH)
    query_grad = stacked[1].reshape(length, DH)
    key_grad = (finals[0] * score_scale).astype(jnp.bfloat16)
    value_grad = finals[1].astype(jnp.bfloat16)
    return (attended, query_grad, key_grad, value_grad)


def attend_heads(query_heads, key_heads, value_heads, grad_heads):
    length = query_heads.shape[1]
    per_device = query_heads.shape[2] // DH
    block_rows = min(512, length)
    gathered = [[], [], [], []]
    for head_index in range(per_device):
        lower = head_index * DH
        upper = lower + DH
        results = head_backward(
            query_heads[0, :, lower:upper],
            key_heads[0, :, lower:upper],
            value_heads[0, :, lower:upper],
            grad_heads[0, :, lower:upper],
            block_rows,
        )
        for position, result in enumerate(results):
            gathered[position].append(result)
    return tuple((jnp.concatenate(group, axis=1)[None] for group in gathered))


def body(queries, key_rows, value_rows, cotangent, out_weight):
    samples = lax.axis_size("dp") * lax.axis_size("fsdp")
    grad_out = jnp.einsum(
        "btd,rd->btr",
        cotangent,
        lax.all_gather(out_weight, "fsdp", axis=0, tiled=True),
        preferred_element_type=jnp.float32,
    ).astype(jnp.bfloat16)
    query_heads, key_heads, value_heads, grad_heads = (
        lax.all_to_all(queries, "seq", split_axis=2, concat_axis=1, tiled=True),
        lax.all_to_all(key_rows, "seq", split_axis=2, concat_axis=1, tiled=True),
        lax.all_to_all(value_rows, "seq", split_axis=2, concat_axis=1, tiled=True),
        lax.all_to_all(grad_out, "seq", split_axis=2, concat_axis=1, tiled=True),
    )
    head_results = attend_heads(query_heads, key_heads, value_heads, grad_heads)
    attended, query_grad, key_grad, value_grad = (
        lax.all_to_all(head_results[0], "seq", split_axis=1, concat_axis=2, tiled=True),
        lax.all_to_all(head_results[1], "seq", split_axis=1, concat_axis=2, tiled=True),
        lax.all_to_all(head_results[2], "seq", split_axis=1, concat_axis=2, tiled=True),
        lax.all_to_all(head_results[3], "seq", split_axis=1, concat_axis=2, tiled=True),
    )
    shares = lax.psum_scatter(
        jnp.einsum("btr,btd->rd", attended, cotangent, preferred_element_type=jnp.float32),
        ("fsdp", "seq"),
        scatter_dimension=0,
        tiled=True,
    )
    shares = lax.psum(shares.astype(jnp.bfloat16), "dp").astype(jnp.float32)
    total = lax.all_gather(shares.astype(jnp.bfloat16), "seq", axis=0, tiled=True).astype(
        shares.dtype
    )
    return (query_grad, key_grad, value_grad, total / samples)


def solution(mesh):
    return jax.shard_map(
        body,
        mesh=mesh,
        in_specs=(
            P(("dp", "fsdp"), "seq", None),
            P(("dp", "fsdp"), "seq", None),
            P(("dp", "fsdp"), "seq", None),
            P(("dp", "fsdp"), "seq", None),
            P("fsdp", None),
        ),
        out_specs=(
            P(("dp", "fsdp"), "seq", None),
            P(("dp", "fsdp"), "seq", None),
            P(("dp", "fsdp"), "seq", None),
            P("fsdp", None),
        ),
        check_vma=False,
    )
```

profile of v0, /device:TPU:0, one launch (start us, length us, event | category | flops | bytes accessed | tf_op | source)
XLA Modules:
  0.0 529.1 jit_solution(7082781794581919626)
XLA Ops:
  8.8 2.4 copy.55
  11.7 11.6 %reduce.1 = bf16[2048,128]{1,0:T(8,128)(2,1)S(1)} reduce(bf16[2048,1,128]{2,1,0:T(2,128)(2,1)S(1)} %bitcast.293, bf16[]{:T(256)} %broadcast.90), dimensions={1}, to_apply=%bitcast.175.reduce_sub_computation | reduce | bytes 1048578
  24.2 4.2 all-to-all-start
  29.2 11.6 %reduce = bf16[2048,128]{1,0:T(8,128)(2,1)S(1)} reduce(bf16[2048,1,128]{2,1,0:T(2,128)(2,1)S(1)} %bitcast.299, bf16[]{:T(256)} %broadcast.90), dimensions={1}, to_apply=%bitcast.177.reduce_sub_computation | reduce | bytes 1048578
  41.6 4.0 all-to-all-start.1
  46.4 11.6 %reduce.2 = bf16[2048,128]{1,0:T(8,128)(2,1)S(1)} reduce(bf16[2048,1,128]{2,1,0:T(2,128)(2,1)S(1)} %bitcast.300, bf16[]{:T(256)} %broadcast.90), dimensions={1}, to_apply=%bitcast.173.reduce_sub_computation | reduce | bytes 1048578
  58.8 3.5 all-to-all-start.3
  65.5 5.5 %all-to-all-done.3 = bf16[2,2,65536]{2,1,0:T(2,128)(2,1)S(1)} async-done(((bf16[2,2,65536]{2,1,0:T(2,128)(2,1)}), bf16[2,2,65536]{2,1,0:T(2,128)(2,1)S(1)}, u32[]{:S(2)}, u32[]{:S(2)}) %all-to-all-start.3) | async-done | bytes 524320 | tf_op jit(solution)/shard_map/all_to_all | solution.py:87
  71.8 1.3 fusion.115
  73.2 1.1 fusion.114
  74.3 1.1 fusion.113
  75.5 1.1 fusion.112
  77.9 1.1 fusion.110
  80.2 1.1 fusion.108
  84.0 2.5 copy.69
  86.5 4.5 reduce.7
  91.0 1.4 reshape.90
  92.4 11.1 %all_to_all.141 = bf16[2,2,65536]{2,1,0:T(2,128)(2,1)} all-to-all(bf16[2,2,65536]{2,1,0:T(2,128)(2,1)S(1)} %reshape.90), channel_id=1, replica_groups=mesh['dp'=4,'fsdp'=4,'seq'=2] {'seq'}, dimensions={0} | all-to-all | bytes 1048576 | tf_op jit(solution)/shard_map/all_to_all | solution.py:92
  103.4 1.4 reshape.91
  105.8 1.3 copy.70
  107.2 8.0 %fusion.49 = f32[2048,2048]{1,0:T(8,128)} fusion(bf16[128,2048]{0,1:T(8,128)(2,1)S(1)} %bitcast.301, bf16[1,128,2048]{2,1,0:T(8,128)(2,1)S(1)} %copy-done), kind=kOutput, calls=%fused_computation.91 | convolution fusion | flops 1073741824 | bytes 17825792 | tf_op jit(solution)/shard_map/btr,btd->rd/dot_general | solution.py:98
  115.2 47.8 %all-gather.3.cloned.1.call-done = bf16[2048,2048]{1,0:T(8,128)(2,1)} async-done(((bf16[512,2048]{1,0:T(8,128)(2,1)}), bf16[2048,2048]{1,0:T(8,128)(2,1)}) %all-gather.3.cloned.1.call-update) | async-done | bytes 8388624 | tf_op jit(solution)/shard_map/all_gather | solution.py:81
  163.1 7.1 %fusion = bf16[1,128,2048]{2,1,0:T(8,128)(2,1)} fusion(bf16[2048,2048]{1,0:T(8,128)(2,1)} %all-gather.3.cloned.1.call-done, bf16[1,128,2048]{2,1,0:T(8,128)(2,1)S(1)} %copy-done), kind=kOutput, calls=%fused_computation.2 | convolution fusion | flops 1074003968 | bytes 9437184 | tf_op jit(solution)/shard_map/btd,rd->btr/dot_general | solution.py:78
  170.1 2.3 copy.59
  172.5 12.4 %reduce.3 = bf16[2048,128]{1,0:T(8,128)(2,1)} reduce(bf16[2048,1,128]{2,1,0:T(2,128)(2,1)S(1)} %bitcast.296, bf16[]{:T(256)} %broadcast.90), dimensions={1}, to_apply=%bitcast.171.reduce_sub_computation | reduce | bytes 1048578
  184.9 1.1 reshape.76
  186.0 17.5 %all_to_all.142 = bf16[2,2,65536]{2,1,0:T(2,128)(2,1)} all-to-all(bf16[2,2,65536]{2,1,0:T(2,128)(2,1)S(1)} %reshape.76), channel_id=1, replica_groups=mesh['dp'=4,'fsdp'=4,'seq'=2] {'seq'}, dimensions={0} | all-to-all | bytes 1048576 | tf_op jit(solution)/shard_map/all_to_all | solution.py:88
  203.5 1.4 reshape.77
  205.8 1.2 copy.60
  209.8 2.5 copy.67
  212.2 4.5 reduce.6
  216.8 2.1 reshape.88
  218.9 3.5 all-to-all-start.6
  222.5 1.3 multiply_reduce_fusion.7
  225.3 1.1 multiply_reduce_fusion.6
  231.4 201.3 %reduce-scatter.2.cloned.1.call-done = f32[256,2048]{1,0:T(8,128)} async-done(((f32[2048,2048]{1,0:T(8,128)}), f32[256,2048]{1,0:T(8,128)}) %reduce-scatter.2.cloned.1.call-update) | async-done | bytes 2097168 | tf_op jit(solution)/shard_map/reduce_scatter | solution.py:97
  432.7 2.7 convert_element_type.240
  437.0 34.3 %all-reduce.2.cloned.1.call-done = bf16[256,2048]{1,0:T(8,128)(2,1)} async-done(((bf16[256,2048]{1,0:T(8,128)(2,1)}), bf16[256,2048]{1,0:T(8,128)(2,1)}) %all-reduce.2.cloned.1.call-update) | async-done | bytes 1048592 | tf_op jit(solution)/shard_map/psum | solution.py:103
  474.2 3.7 reduce.4
  477.9 1.1 reshape.84
  479.9 3.5 all-to-all-start.4
  485.1 2.5 copy.65
  487.6 3.7 reduce.5
  491.3 1.1 reshape.86
  492.4 5.0 all-to-all-done.4
  497.4 3.5 all-to-all-start.5
  504.8 9.8 %all-to-all-done.5 = bf16[2,2,65536]{2,1,0:T(2,128)(2,1)S(1)} async-done(((bf16[2,2,65536]{2,1,0:T(2,128)(2,1)}), bf16[2,2,65536]{2,1,0:T(2,128)(2,1)S(1)}, u32[]{:S(2)}, u32[]{:S(2)}) %all-to-all-start.5) | async-done | bytes 524320 | tf_op jit(solution)/shard_map/all_to_all | solution.py:94
  516.9 4.2 convert_multiply_fusion
  (132 shorter events, 38.7 us)
Async XLA Ops:
  8.0 99.2 %copy-start = (bf16[1,128,2048]{2,1,0:T(8,128)(2,1)S(1)}, bf16[1,128,2048]{2,1,0:T(8,128)(2,1)}, u32[]{:S(2)}) copy-start(bf16[1,128,2048]{2,1,0:T(8,128)(2,1)} %param.8) | copy-start | bytes 1572868
  8.0 20.4 %copy-start.6 = (bf16[1,128,2048]{2,1,0:T(8,128)(2,1)S(1)}, bf16[1,128,2048]{2,1,0:T(8,128)(2,1)}, u32[]{:S(2)}) copy-start(bf16[1,128,2048]{2,1,0:T(8,128)(2,1)} %param.6) | copy-start | bytes 1572868
  8.0 155.0 %all-gather.3.cloned.1.call-start = ((), (), s32[]{:S(2)}) async-start(), calls=%async_computation.9 | async-start | bytes 10485760 | tf_op jit(solution)/shard_map/all_gather | solution.py:81
  11.7 33.9 %copy-start.7 = (bf16[1,128,2048]{2,1,0:T(8,128)(2,1)S(1)}, bf16[1,128,2048]{2,1,0:T(8,128)(2,1)}, u32[]{:S(2)}) copy-start(bf16[1,128,2048]{2,1,0:T(8,128)(2,1)} %param.7) | copy-start | bytes 1572868
  24.2 17.4 %all-to-all-start = ((bf16[2,2,65536]{2,1,0:T(2,128)(2,1)}), bf16[2,2,65536]{2,1,0:T(2,128)(2,1)S(1)}, u32[]{:S(2)}, u32[]{:S(2)}) async-start(bf16[2,2,65536]{2,1,0:T(2,128)(2,1)} %reshape.80), calls=%async_computation | async-start | bytes 1048576 | tf_op jit(solution)/shard_map/all_to_all | solution.py:85
  41.6 17.2 %all-to-all-start.1 = ((bf16[2,2,65536]{2,1,0:T(2,128)(2,1)}), bf16[2,2,65536]{2,1,0:T(2,128)(2,1)S(1)}, u32[]{:S(2)}, u32[]{:S(2)}) async-start(bf16[2,2,65536]{2,1,0:T(2,128)(2,1)} %reshape.82), calls=%async_computation.1 | async-start | bytes 1048576 | tf_op jit(solution)/shard_map/all_to_all | solution.py:86
  58.8 12.2 %all-to-all-start.3 = ((bf16[2,2,65536]{2,1,0:T(2,128)(2,1)}), bf16[2,2,65536]{2,1,0:T(2,128)(2,1)S(1)}, u32[]{:S(2)}, u32[]{:S(2)}) async-start(bf16[2,2,65536]{2,1,0:T(2,128)(2,1)} %reshape.78), calls=%async_computation.3 | async-start | bytes 1048576 | tf_op jit(solution)/shard_map/all_to_all | solution.py:87
  62.3 370.3 %reduce-scatter.2.cloned.1.call-start = ((), (), s32[]{:S(2)}) async-start(), calls=%async_computation.10 | async-start | bytes 18874368 | tf_op jit(solution)/shard_map/reduce_scatter | solution.py:97
  71.8 11.1 %copy-start.13 = (bf16[1,2,128,1024]{3,2,1,0:T(8,128)(2,1)}, bf16[1,2,128,1024]{3,2,1,0:T(8,128)(2,1)S(1)}, u32[]{:S(2)}) copy-start(bf16[1,2,128,1024]{3,2,1,0:T(8,128)(2,1)S(1)} %copy.62) | copy-start | bytes 1572868
  81.3 1.6 copy-start.3
  83.2 0.8 copy-start.11
  172.5 34.6 %copy-start.4 = (f32[256,256]{0,1:T(8,128)S(1)}, f32[256,256]{0,1:T(8,128)}, u32[]{:S(2)}) copy-start(f32[256,256]{0,1:T(8,128)} %copy-done.3) | copy-start | bytes 786436
  207.1 1.9 copy-start.15
  208.7 16.1 %copy-start.2 = (bf16[1,2,128,1024]{3,2,1,0:T(8,128)(2,1)S(1)}, bf16[1,2,128,1024]{3,2,1,0:T(8,128)(2,1)}, u32[]{:S(2)}) copy-start(bf16[1,2,128,1024]{3,2,1,0:T(8,128)(2,1)} %copy.56) | copy-start | bytes 1572868
  209.0 0.8 copy-start.12
  216.8 8.3 %copy-start.5 = (bf16[1,2,128,1024]{3,2,1,0:T(8,128)(2,1)S(1)}, bf16[1,2,128,1024]{3,2,1,0:T(8,128)(2,1)}, u32[]{:S(2)}) copy-start(bf16[1,2,128,1024]{3,2,1,0:T(8,128)(2,1)} %copy.58) | copy-start | bytes 1572868
  218.9 261.0 %all-to-all-start.6 = ((bf16[2,2,65536]{2,1,0:T(2,128)(2,1)}), bf16[2,2,65536]{2,1,0:T(2,128)(2,1)S(1)}, u32[]{:S(2)}, u32[]{:S(2)}) async-start(bf16[2,2,65536]{2,1,0:T(2,128)(2,1)} %reshape.88), calls=%async_computation.6 | async-start | bytes 1048576 | tf_op jit(solution)/shard_map/all_to_all | solution.py:95
  222.4 248.9 %all-reduce.2.cloned.1.call-start = ((), (), s32[]{:S(2)}) async-start(), calls=%async_computation.11 | async-start | bytes 2097152 | tf_op jit(solution)/shard_map/psum | solution.py:103
  222.4 4.5 copy-start.14
  222.5 4.5 copy-start.16
  228.4 0.8 copy-start.8
  229.4 0.8 copy-start.10
  230.2 205.5 %copy-start.9 = (bf16[256,1024]{0,1:T(8,128)(2,1)S(1)}, bf16[256,1024]{0,1:T(8,128)(2,1)}, u32[]{:S(2)}) copy-start(bf16[256,1024]{0,1:T(8,128)(2,1)} %copy-done.8) | copy-start | bytes 1572868
  435.4 81.5 %all-gather.5.cloned.1.call-start = ((), (), s32[]{:S(2)}) async-start(), calls=%async_computation.12 | async-start | bytes 3145728 | tf_op jit(solution)/shard_map/all_gather | solution.py:104
  479.9 17.5 %all-to-all-start.4 = ((bf16[2,2,65536]{2,1,0:T(2,128)(2,1)}), bf16[2,2,65536]{2,1,0:T(2,128)(2,1)S(1)}, u32[]{:S(2)}, u32[]{:S(2)}) async-start(bf16[2,2,65536]{2,1,0:T(2,128)(2,1)} %reshape.84), calls=%async_computation.4 | async-start | bytes 1048576 | tf_op jit(solution)/shard_map/all_to_all | solution.py:93
  497.4 17.3 %all-to-all-start.5 = ((bf16[2,2,65536]{2,1,0:T(2,128)(2,1)}), bf16[2,2,65536]{2,1,0:T(2,128)(2,1)S(1)}, u32[]{:S(2)}, u32[]{:S(2)}) async-start(bf16[2,2,65536]{2,1,0:T(2,128)(2,1)} %reshape.86), calls=%async_computation.5 | async-start | bytes 1048576 | tf_op jit(solution)/shard_map/all_to_all | solution.py:94
  515.3 5.7 %copy-start.1 = (bf16[1,128,2048]{2,1,0:T(8,128)(2,1)S(1)}, bf16[1,128,2048]{2,1,0:T(8,128)(2,1)}, u32[]{:S(2)}) copy-start(bf16[1,128,2048]{2,1,0:T(8,128)(2,1)} %param.8) | copy-start | bytes 1572868
Sparse Core Ops, SparseCore 0:
  10.4 152.5 all-gather.2
Sparse Core Ops, SparseCore 1:
  115.3 317.3 reduce-scatter.1
  435.6 35.7 all-reduce.1
  472.7 44.1 all-gather.4
where the time goes:
time: 538 us; the launch traced here: 529 us
  waiting for transfers between devices  305 us (57%)
  other arithmetic  73.5 us (14%)
  local copies, waits for them, and re-layouts  44.6 us (8%)
  matrix products  38.3 us (7%)
  blocking collectives  28.6 us (5%)
  starting transfers between devices  22.6 us (4%)
  between operations  16.8 us (3%)
    reduce_scatter x1, waiting for transfers between devices, body(): lax.psum_scatter(jnp.einsum('btr,btd->rd', attended, cotangent, preferred...  201 us
    unnamed x8, other arithmetic  63.6 us
    all_gather x1, waiting for transfers between devices, body(): lax.all_gather(out_weight, 'fsdp', axis=0, tiled=True)  47.8 us
    psum x1, waiting for transfers between devices, body(): shares = lax.psum(shares.astype(jnp.bfloat16), 'dp').astype(jnp.float32)  34.3 us
    unnamed x65, local copies, waits for them, and re-layouts  28.2 us
    all_to_all x1, blocking collectives, body(): lax.all_to_all(grad_out, 'seq', split_axis=2, concat_axis=1, tiled=True)  17.5 us
    all_to_all x1, blocking collectives, body(): lax.all_to_all(head_results[0], 'seq', split_axis=1, concat_axis=2, tiled...  11.1 us
  transfers between devices with their start and end apart: 10, of which 7 were waited for; matrix products, arithmetic and copies ran while one was open for 28% of the time, Pallas kernels for 0%

commit v1 on v0

--- a/solution.py
+++ b/solution.py
@@ -1,9 +1,16 @@
+import functools
+
 import jax
 import jax.numpy as jnp
 from jax import lax
+from jax.experimental import pallas as pl
+from jax.experimental.pallas import tpu as pltpu
 from jax.sharding import PartitionSpec as P
 
 DH = 128
+CHUNKS = 4
+F32 = jnp.float32
+BF16 = jnp.bfloat16
 
 
 def head_backward(query_head, key_head, value_head, grad_head, block_rows):
@@ -107,9 +114,414 @@
     return (query_grad, key_grad, value_grad, total / samples)
 
 
+def dot_nn(a, b):
+    return lax.dot_general(a, b, (((1,), (0,)), ((), ())), preferred_element_type=F32)
+
+
+def dot_nt(a, b):
+    return lax.dot_general(a, b, (((1,), (1,)), ((), ())), preferred_element_type=F32)
+
+
+def dot_tn(a, b):
+    return lax.dot_general(a, b, (((0,), (0,)), ((), ())), preferred_element_type=F32)
+
+
+def fused_kernel(
+    nf,
+    q_ref,
+    k_ref,
+    v_ref,
+    c_ref,
+    w_ref,
+    qg_ref,
+    kg_ref,
+    vg_ref,
+    wg_ref,
+    cot,
+    keys,
+    vals,
+    go_out,
+    go_in,
+    at_out,
+    at_in,
+    probs,
+    kv_out,
+    kv_in,
+    kv_own,
+    acc,
+    core_out,
+    core_in,
+    y_out,
+    y_in,
+    x_out,
+    x_in,
+    final,
+    cot_send,
+    cot_recv,
+    pair_send,
+    pair_recv,
+    go_send,
+    go_recv,
+    at_send,
+    at_recv,
+    kv_send,
+    kv_recv,
+    rs_send,
+    rs_recv,
+    ag_send,
+    ag_recv,
+):
+    tokens, width = c_ref.shape
+    rows = w_ref.shape[0]
+    group_heads = rows // DH
+    scale = DH ** (-0.5)
+    dp = lax.axis_index("dp")
+    f = lax.axis_index("fsdp")
+    s = lax.axis_index("seq")
+    core = dp % 2
+    half = dp // 2
+    sibling = {"dp": half * 2 + (1 - core)}
+    across = {"dp": (1 - half) * 2 + core}
+    partner = {"seq": 1 - s}
+
+    def remote(src, dst, send, recv, device):
+        return pltpu.make_async_remote_copy(
+            src_ref=src,
+            dst_ref=dst,
+            send_sem=send,
+            recv_sem=recv,
+            device_id=device,
+            device_id_type=pl.DeviceIdType.MESH,
+        )
+
+    barrier = pltpu.get_barrier_semaphore()
+    for device in (sibling, across, partner):
+        pl.semaphore_signal(
+            barrier, inc=1, device_id=device, device_id_type=pl.DeviceIdType.MESH
+        )
+    for step in range(1, nf):
+        pl.semaphore_signal(
+            barrier,
+            inc=1,
+            device_id={"fsdp": (f + step) % nf},
+            device_id_type=pl.DeviceIdType.MESH,
+        )
+    pl.semaphore_wait(barrier, 3 + nf - 1)
+
+    def cot_up(j):
+        return remote(cot.at[j], cot.at[j], cot_send.at[0, j], cot_recv.at[j], {"fsdp": f + 1})
+
+    def cot_down(j):
+        return remote(cot.at[j], cot.at[j], cot_send.at[1, j], cot_recv.at[j], {"fsdp": f - 1})
+
+    def go_copy(j, peer):
+        return remote(go_out.at[j], go_in.at[f], go_send.at[j], go_recv.at[f], {"fsdp": peer})
+
+    def at_copy(j, peer):
+        return remote(at_out.at[j], at_in.at[f], at_send.at[j], at_recv.at[f], {"fsdp": peer})
+
+    def kv_copy(which, g):
+        return remote(
+            kv_out.at[which, g],
+            kv_in.at[which, g],
+            kv_send.at[which, g],
+            kv_recv.at[which, g],
+            partner,
+        )
+
+    def wait_into(ref, sem):
+        pltpu.make_async_copy(ref, ref, sem).wait()
+
+    cot[f] = c_ref[...]
+
+    @pl.when(f + 1 < nf)
+    def _():
+        cot_up(f).start()
+
+    @pl.when(f > 0)
+    def _():
+        cot_down(f).start()
+
+    keys[0] = k_ref[...]
+    vals[0] = v_ref[...]
+    key_copy = remote(keys.at[0], keys.at[1], pair_send.at[0], pair_recv.at[0], partner)
+    val_copy = remote(vals.at[0], vals.at[1], pair_send.at[1], pair_recv.at[1], partner)
+    key_copy.start()
+    val_copy.start()
+
+    def project(j):
+        return dot_nt(cot[j], w_ref[...]).astype(BF16)
+
+    go_in[f] = project(f)
+
+    def visit_peers(first, last, action):
+        def step(i, carry):
+            d = i // 2
+            j = f + d * (1 - 2 * (i % 2))
+
+            @pl.when((j >= 0) & (j < nf))
+            def _():
+                action(j)
+
+            return carry
+
+        lax.fori_loop(2 * first, 2 * last, step, 0)
+
+    def take_cot(j):
+        wait_into(cot.at[j], cot_recv.at[j])
+
+        @pl.when((j < f) & (f + 1 < nf))
+        def _():
+            cot_up(j).start()
+
+        @pl.when((j > f) & (f > 0))
+        def _():
+            cot_down(j).start()
+
+        go_out[j] = project(j)
+        go_copy(j, j).start()
+
+    visit_peers(1, nf - 1, take_cot)
+
+    key_copy.wait()
+    val_copy.wait()
+
+    def soften(g, carry):
+        base = g * rows
+        for t in range(group_heads):
+            cols = pl.ds(pl.multiple_of(base + t * DH, DH), DH)
+            kh = keys[:, :, cols].reshape(2 * tokens, DH)
+            vh = vals[:, :, cols].reshape(2 * tokens, DH)
+            scores = dot_nt(q_ref[:, cols], kh) * scale
+            highest = jnp.max(scores, axis=1, keepdims=True)
+            expanded = jnp.exp(scores - highest)
+            weights = expanded / jnp.sum(expanded, axis=1, keepdims=True)
+            probs[g * group_heads + t] = weights
+            at_out[g, :, t * DH : (t + 1) * DH] = dot_nn(weights.astype(BF16), vh).astype(BF16)
+
+        @pl.when(g == f)
+        def _():
+            at_in[f] = at_out[f]
+
+        @pl.when(g != f)
+        def _():
+            at_copy(g, g).start()
+
+        return carry
+
+    lax.fori_loop(0, nf, soften, 0)
+
+    def differentiate(g):
+        base = g * rows
+        for t in range(group_heads):
+            cols = pl.ds(pl.multiple_of(base + t * DH, DH), DH)
+            inner = slice(t * DH, (t + 1) * DH)
+            kh = keys[:, :, cols].reshape(2 * tokens, DH)
+            vh = vals[:, :, cols].reshape(2 * tokens, DH)
+            qh = q_ref[:, cols]
+            gh = go_in[g, :, inner]
+            weights = probs[g * group_heads + t]
+            grad_weights = dot_nt(gh, vh)
+            delta = jnp.sum(weights * grad_weights, axis=1, keepdims=True)
+            grad_scores = (weights * (grad_weights - delta)).astype(BF16)
+            qg_ref[:, cols] = (dot_nn(grad_scores, kh) * scale).astype(BF16)
+            kg = dot_tn(grad_scores, qh) * scale
+            vg = dot_tn(weights.astype(BF16), gh)
+            kv_own[0, g, :, inner] = kg[:tokens]
+            kv_own[1, g, :, inner] = vg[:tokens]
+            kv_out[0, g, :, inner] = kg[tokens:].astype(BF16)
+            kv_out[1, g, :, inner] = vg[tokens:].astype(BF16)
+        kv_copy(0, g).start()
+        kv_copy(1, g).start()
+
+    def take_go(j):
+        wait_into(go_in.at[j], go_recv.at[j])
+        differentiate(j)
+
+    differentiate(f)
+    visit_peers(nf - 1, nf, take_cot)
+    visit_peers(1, nf - 1, take_go)
+
+    visit_peers(1, nf, lambda j: wait_into(at_in.at[j], at_recv.at[j]))
+
+    part = width // CHUNKS
+    core_rows, y_rows, x_rows = rows // 2, rows // 4, rows // 8
+    core_base = pl.multiple_of(core * core_rows, core_rows)
+    core_other = pl.multiple_of((1 - core) * core_rows, core_rows)
+    y_base = pl.multiple_of(half * y_rows, y_rows)
+    y_other = pl.multiple_of((1 - half) * y_rows, y_rows)
+    x_base = pl.multiple_of(s * x_rows, x_rows)
+    x_other = pl.multiple_of((1 - s) * x_rows, x_rows)
+
+    def reduce_copy(stage, c):
+        src, dst, device = (
+            (core_out, core_in, sibling),
+            (y_out, y_in, across),
+            (x_out, x_in, partner),
+        )[stage]
+        return remote(src.at[c], dst.at[c], rs_send.at[stage, c], rs_recv.at[stage, c], device)
+
+    def gather_copy(stage, c):
+        base, count, device = (
+            (core_base, core_rows, sibling),
+            (core_base + y_base, y_rows, across),
+            (core_base + y_base + x_base, x_rows, partner),
+        )[stage]
+        block = final.at[c, pl.ds(pl.multiple_of(base, count), count)]
+        return remote(block, block, ag_send.at[stage, c], ag_recv.at[stage, c], device)
+
+    for c in range(CHUNKS):
+        acc[c] = dot_tn(
+            at_in[...].reshape(nf * tokens, rows),
+            cot[:, :, c * part : (c + 1) * part].reshape(nf * tokens, part),
+        )
+        core_out[c] = acc[c, pl.ds(core_other, core_rows)].astype(BF16)
+        reduce_copy(0, c).start()
+
+    def reduce_core(c):
+        reduce_copy(0, c).wait_recv()
+        acc[c, pl.ds(core_base, core_rows)] += core_in[c].astype(F32)
+        y_out[c] = acc[c, pl.ds(core_base + y_other, y_rows)].astype(BF16)
+        reduce_copy(1, c).start()
+
+    def reduce_y(c):
+        reduce_copy(1, c).wait_recv()
+        acc[c, pl.ds(core_base + y_base, y_rows)] += y_in[c].astype(F32)
+        x_out[c] = acc[c, pl.ds(core_base + y_base + x_other, x_rows)].astype(BF16)
+        reduce_copy(2, c).start()
+
+    def reduce_x(c):
+        reduce_copy(2, c).wait_recv()
+        mine = pl.ds(core_base + y_base + x_base, x_rows)
+        final[c, mine] = (acc[c, mine] + x_in[c].astype(F32)).astype(BF16)
+        gather_copy(2, c).start()
+
+    def gather_x(c):
+        gather_copy(2, c).wait()
+        gather_copy(1, c).start()
+
+    def gather_y(c):
+        gather_copy(1, c).wait()
+        gather_copy(0, c).start()
+
+    def gather_core(c):
+        gather_copy(0, c).wait()
+        wg_ref[:, c * part : (c + 1) * part] = final[c]
+
+    for c in range(CHUNKS):
+        reduce_core(c)
+
+    visit_peers(nf - 1, nf, take_go)
+
+    for stage in (reduce_y, reduce_x, gather_x, gather_y):
+        for c in range(CHUNKS):
+            stage(c)
+
+    def finish(g):
+        cols = pl.ds(pl.multiple_of(g * rows, rows), rows)
+        for which, out in ((0, kg_ref), (1, vg_ref)):
+            kv_copy(which, g).wait()
+            out[:, cols] = (kv_own[which, g] + kv_in[which, g].astype(F32)).astype(BF16)
+
+    finish(f)
+    visit_peers(1, nf, finish)
+
+    for c in range(CHUNKS):
+        gather_core(c)
+        for stage in range(3):
+            reduce_copy(stage, c).wait_send()
+
+    def drain(j):
+        go_copy(j, j).wait_send()
+        at_copy(j, j).wait_send()
+
+        @pl.when((j < f) & (f + 1 < nf))
+        def _():
+            cot_up(j).wait_send()
+
+        @pl.when((j > f) & (f > 0))
+        def _():
+            cot_down(j).wait_send()
+
+    visit_peers(1, nf, drain)
+
+    @pl.when(f + 1 < nf)
+    def _():
+        cot_up(f).wait_send()
+
+    @pl.when(f > 0)
+    def _():
+        cot_down(f).wait_send()
+
+
+def fused_body(nf, queries, key_rows, value_rows, cotangent, out_weight):
+    samples = lax.axis_size("dp") * nf
+    tokens, heads_width = queries.shape[1:]
+    rows, width = out_weight.shape
+    part = width // CHUNKS
+    vmem = pl.BlockSpec(memory_space=pltpu.VMEM)
+    dma = pltpu.SemaphoreType.DMA
+    outs = pl.pallas_call(
+        functools.partial(fused_kernel, nf),
+        out_shape=(
+            jax.ShapeDtypeStruct((tokens, heads_width), BF16),
+            jax.ShapeDtypeStruct((tokens, heads_width), BF16),
+            jax.ShapeDtypeStruct((tokens, heads_width), BF16),
+            jax.ShapeDtypeStruct((rows, width), BF16),
+        ),
+        in_specs=[vmem] * 5,
+        out_specs=[vmem] * 4,
+        scratch_shapes=[
+            pltpu.VMEM((nf, tokens, width), BF16),
+            pltpu.VMEM((2, tokens, heads_width), BF16),
+            pltpu.VMEM((2, tokens, heads_width), BF16),
+            pltpu.VMEM((nf, tokens, rows), BF16),
+            pltpu.VMEM((nf, tokens, rows), BF16),
+            pltpu.VMEM((nf, tokens, rows), BF16),
+            pltpu.VMEM((nf, tokens, rows), BF16),
+            pltpu.VMEM((heads_width // DH, tokens, 2 * tokens), F32),
+            pltpu.VMEM((2, nf, tokens, rows), BF16),
+            pltpu.VMEM((2, nf, tokens, rows), BF16),
+            pltpu.VMEM((2, nf, tokens, rows), F32),
+            pltpu.VMEM((CHUNKS, rows, part), F32),
+            pltpu.VMEM((CHUNKS, rows // 2, part), BF16),
+            pltpu.VMEM((CHUNKS, rows // 2, part), BF16),
+            pltpu.VMEM((CHUNKS, rows // 4, part), BF16),
+            pltpu.VMEM((CHUNKS, rows // 4, part), BF16),
+            pltpu.VMEM((CHUNKS, rows // 8, part), BF16),
+            pltpu.VMEM((CHUNKS, rows // 8, part), BF16),
+            pltpu.VMEM((CHUNKS, rows, part), BF16),
+            dma((2, nf)),
+            dma((nf,)),
+            dma((2,)),
+            dma((2,)),
+            dma((nf,)),
+            dma((nf,)),
+            dma((nf,)),
+            dma((nf,)),
+            dma((2, nf)),
+            dma((2, nf)),
+            dma((3, CHUNKS)),
+            dma((3, CHUNKS)),
+            dma((3, CHUNKS)),
+            dma((3, CHUNKS)),
+        ],
+        compiler_params=pltpu.CompilerParams(
+            collective_id=0, has_side_effects=True, vmem_limit_bytes=48 * 1024 * 1024
+        ),
+    )(queries[0], key_rows[0], value_rows[0], cotangent[0], out_weight)
+    return (outs[0][None], outs[1][None], outs[2][None], outs[3].astype(F32) / samples)
+
+
+def pick_body(mesh):
+    if mesh.shape["seq"] == 2 and mesh.shape["dp"] == 4:
+        return functools.partial(fused_body, mesh.shape["fsdp"])
+    return body
+
+
 def solution(mesh):
     return jax.shard_map(
-        body,
+        pick_body(mesh),
         mesh=mesh,
         in_specs=(
             P(("dp", "fsdp"), "seq", None),

time: 538 us -> 105 us (0.20); the launches traced: 529 us -> 105 us
  waiting for transfers between devices: 305 us -> 0 us
  Pallas kernels: 0 us -> 95.1 us
  other arithmetic: 73.5 us -> 2.58 us
  matrix products: 38.3 us -> 0 us
  local copies, waits for them, and re-layouts: 44.6 us -> 6.54 us
  blocking collectives: 28.6 us -> 0 us
  starting transfers between devices: 22.6 us -> 0 us
  between operations: 16.8 us -> 0.65 us
    reduce_scatter x1 -> x0, waiting for transfers between devices: 201 us -> none  [body(): lax.psum_scatter(jnp.einsum('btr,btd->rd', attended, cotangent, preferred...]
    pallas_call x0 -> x1, Pallas kernels: none -> 95.1 us  [fused_body(): pl.pallas_call(functools.partial(fused_kernel, nf), out_shape=(jax.ShapeD...]
    unnamed x8 -> x0, other arithmetic: 63.6 us -> none
    all_gather x2 -> x0, waiting for transfers between devices: 48.1 us -> none  [the longest x1 47.8 us: body(): lax.all_gather(out_weight, 'fsdp', axis=0, tiled=True)]
    dot_general x50 -> x0, matrix products: 38.3 us -> none  [the longest x8 8.91 us: visit(): jnp.einsum('qd,kd->qk', query_block, key_head, preferred_element_type=jnp...]
    psum x1 -> x0, waiting for transfers between devices: 34.3 us -> none  [body(): shares = lax.psum(shares.astype(jnp.bfloat16), 'dp').astype(jnp.float32)]
    all_to_all x2 -> x0, blocking collectives: 28.6 us -> none  [the longest x1 17.5 us: body(): lax.all_to_all(grad_out, 'seq', split_axis=2, concat_axis=1, tiled=True)]
    all_to_all x6 -> x0, starting transfers between devices: 22.2 us -> none  [the longest x1 4.21 us: body(): lax.all_to_all(queries, 'seq', split_axis=2, concat_axis=1, tiled=True)]
  transfers between devices with their start and end apart: 10 -> 0, of which waited for: 7 -> 0; matrix products, arithmetic and copies ran while one was open for 28% -> 0% of each run, Pallas kernels for 0% -> 0%
where the time goes in v1:
time: 105 us
  Pallas kernels  95.1 us (91%)
  local copies, waits for them, and re-layouts  6.54 us (6%)
  other arithmetic  2.58 us (2%)
    pallas_call x1, Pallas kernels, fused_body(): pl.pallas_call(functools.partial(fused_kernel, nf), out_shape=(jax.ShapeD...  95.1 us
    unnamed x11, local copies, waits for them, and re-layouts  6.54 us
    div x1, other arithmetic, fused_body(): outs[3].astype(F32) / samples  2.58 us

profile of v1, /device:TPU:0, one launch (start us, length us, event | category | flops | bytes accessed | tf_op | source)
XLA Modules:
  0.0 104.9 jit_solution(10028900940624179529)
XLA Ops:
  0.6 0.0 copy-start
  0.6 1.0 copy-done
  1.7 0.0 copy-start.1
  1.7 1.0 copy-done.1
  2.7 0.0 copy-start.2
  2.7 1.0 copy-done.2
  3.8 0.0 copy-start.3
  3.8 1.0 copy-done.3
  4.8 95.1 %shard_map.84 = (bf16[128,2048]{1,0:T(8,128)(2,1)S(1)}, bf16[128,2048]{1,0:T(8,128)(2,1)S(1)}, bf16[128,2048]{1,0:T(8,128)(2,1)S(1)}, bf16[512,2048]{1,0:T(8,128)(2,1)S(1)}) custom-call(bf16[128,2048]{1,0:T(8,128)(2,1)S(1)} %bitcast.10, bf16[128,2048]{1,0:T(8,128)(2,1)S(1)} %bitcast.11, bf16[128,2048]{1,0:T(8,128)(2,1)S(1)} %bitcast.12, ...), custom_call_target="tpu_custom_call" | custom-call | tf_op jit(solution)/shard_map/pallas_call | solution.py:464
  99.9 2.6 %convert_multiply_fusion = f32[512,2048]{1,0:T(8,128)} fusion(bf16[512,2048]{1,0:T(8,128)(2,1)S(1)} %get-tuple-element.11), kind=kLoop, calls=%fused_computation | loop fusion | flops 2097152 | bytes 6291456 | tf_op jit(solution)/shard_map/div | solution.py:513
  102.5 0.8 copy.12
  103.3 0.8 copy.13
  104.1 0.8 copy.14
Async XLA Ops:
  0.6 1.0 copy-start
  1.7 1.0 copy-start.1
  2.7 1.0 copy-start.2
  3.8 1.0 copy-start.3

commit v2 on v1

--- a/solution.py
+++ b/solution.py
@@ -9,6 +9,8 @@
 
 DH = 128
 CHUNKS = 4
+X_FIRST = (3,)
+STORES = 8
 F32 = jnp.float32
 BF16 = jnp.bfloat16
 
@@ -128,15 +130,15 @@
 
 def fused_kernel(
     nf,
-    q_ref,
-    k_ref,
-    v_ref,
-    c_ref,
-    w_ref,
-    qg_ref,
-    kg_ref,
-    vg_ref,
-    wg_ref,
+    q_hbm,
+    k_hbm,
+    v_hbm,
+    c_hbm,
+    w_hbm,
+    qg_hbm,
+    kg_hbm,
+    vg_hbm,
+    wg_hbm,
     cot,
     keys,
     vals,
@@ -156,6 +158,14 @@
     x_out,
     x_in,
     final,
+    q_ref,
+    w_ref,
+    qg_ref,
+    kg_ref,
+    vg_ref,
+    load_sem,
+    store_sem,
+    wide_sem,
     cot_send,
     cot_recv,
     pair_send,
@@ -171,7 +181,7 @@
     ag_send,
     ag_recv,
 ):
-    tokens, width = c_ref.shape
+    tokens, width = c_hbm.shape
     rows = w_ref.shape[0]
     group_heads = rows // DH
     scale = DH ** (-0.5)
@@ -194,6 +204,21 @@
             device_id_type=pl.DeviceIdType.MESH,
         )
 
+    loads = [
+        pltpu.make_async_copy(src, dst, load_sem.at[i])
+        for i, (src, dst) in enumerate(
+            (
+                (c_hbm, cot.at[f]),
+                (w_hbm, w_ref),
+                (k_hbm, keys.at[0]),
+                (v_hbm, vals.at[0]),
+                (q_hbm, q_ref),
+            )
+        )
+    ]
+    for load in loads:
+        load.start()
+
     barrier = pltpu.get_barrier_semaphore()
     for device in (sibling, across, partner):
         pl.semaphore_signal(
@@ -232,26 +257,38 @@
     def wait_into(ref, sem):
         pltpu.make_async_copy(ref, ref, sem).wait()
 
-    cot[f] = c_ref[...]
+    own_up = remote(c_hbm, cot.at[f], cot_send.at[0, f], cot_recv.at[f], {"fsdp": f + 1})
+    own_down = remote(c_hbm, cot.at[f], cot_send.at[1, f], cot_recv.at[f], {"fsdp": f - 1})
 
     @pl.when(f + 1 < nf)
     def _():
-        cot_up(f).start()
+        own_up.start()
 
     @pl.when(f > 0)
     def _():
-        cot_down(f).start()
-
-    keys[0] = k_ref[...]
-    vals[0] = v_ref[...]
-    key_copy = remote(keys.at[0], keys.at[1], pair_send.at[0], pair_recv.at[0], partner)
-    val_copy = remote(vals.at[0], vals.at[1], pair_send.at[1], pair_recv.at[1], partner)
-    key_copy.start()
-    val_copy.start()
+        own_down.start()
+
+    def pair_copy(which, i):
+        g = (f + 1 + i) % nf
+        cols = pl.ds(pl.multiple_of(g * rows, rows), rows)
+        src, dst = ((k_hbm, keys), (v_hbm, vals))[which]
+        return remote(
+            src.at[:, cols],
+            dst.at[1, :, cols],
+            pair_send.at[which, i],
+            pair_recv.at[which, i],
+            partner,
+        )
+
+    for i in range(nf):
+        pair_copy(0, i).start()
+        pair_copy(1, i).start()
 
     def project(j):
         return dot_nt(cot[j], w_ref[...]).astype(BF16)
 
+    loads[0].wait()
+    loads[1].wait()
     go_in[f] = project(f)
 
     def visit_peers(first, last, action):
@@ -281,13 +318,11 @@
         go_out[j] = project(j)
         go_copy(j, j).start()
 
-    visit_peers(1, nf - 1, take_cot)
-
-    key_copy.wait()
-    val_copy.wait()
-
-    def soften(g, carry):
+    def soften(i):
+        g = (f + 1 + i) % nf
         base = g * rows
+        pair_copy(0, i).wait()
+        pair_copy(1, i).wait()
         for t in range(group_heads):
             cols = pl.ds(pl.multiple_of(base + t * DH, DH), DH)
             kh = keys[:, :, cols].reshape(2 * tokens, DH)
@@ -299,17 +334,11 @@
             probs[g * group_heads + t] = weights
             at_out[g, :, t * DH : (t + 1) * DH] = dot_nn(weights.astype(BF16), vh).astype(BF16)
 
-        @pl.when(g == f)
-        def _():
+        if i == nf - 1:
             at_in[f] = at_out[f]
-
-        @pl.when(g != f)
-        def _():
+        else:
             at_copy(g, g).start()
 
-        return carry
-
-    lax.fori_loop(0, nf, soften, 0)
 
     def differentiate(g):
         base = g * rows
@@ -338,61 +367,80 @@
         wait_into(go_in.at[j], go_recv.at[j])
         differentiate(j)
 
+    for load in loads[2:]:
+        load.wait()
+    soften(0)
+    for d in range(1, nf):
+        visit_peers(d, d + 1, take_cot)
+        soften(d)
     differentiate(f)
-    visit_peers(nf - 1, nf, take_cot)
     visit_peers(1, nf - 1, take_go)
 
     visit_peers(1, nf, lambda j: wait_into(at_in.at[j], at_recv.at[j]))
 
     part = width // CHUNKS
-    core_rows, y_rows, x_rows = rows // 2, rows // 4, rows // 8
-    core_base = pl.multiple_of(core * core_rows, core_rows)
-    core_other = pl.multiple_of((1 - core) * core_rows, core_rows)
-    y_base = pl.multiple_of(half * y_rows, y_rows)
-    y_other = pl.multiple_of((1 - half) * y_rows, y_rows)
-    x_base = pl.multiple_of(s * x_rows, x_rows)
-    x_other = pl.multiple_of((1 - s) * x_rows, x_rows)
+    core_rows, mid_rows, low_rows = rows // 2, rows // 4, rows // 8
+
+    def bases(c):
+        first, second = (s, half) if c in X_FIRST else (half, s)
+        mid = core * core_rows + first * mid_rows
+        mid_other = core * core_rows + (1 - first) * mid_rows
+        low = mid + second * low_rows
+        low_other = mid + (1 - second) * low_rows
+        return mid, mid_other, low, low_other
+
+    def span(base, count):
+        return pl.ds(pl.multiple_of(base, count), count)
+
+    def device_of(stage, c):
+        if stage == 0:
+            return sibling
+        return partner if (stage == 1) == (c in X_FIRST) else across
 
     def reduce_copy(stage, c):
-        src, dst, device = (
-            (core_out, core_in, sibling),
-            (y_out, y_in, across),
-            (x_out, x_in, partner),
+        src, dst = ((core_out, core_in), (y_out, y_in), (x_out, x_in))[stage]
+        device = device_of(stage, c)
+        return remote(src.at[c], dst.at[c], rs_send.at[stage, c], rs_recv.at[stage, c], device)
+
+    def gather_copy(stage, c):
+        base, count = (
+            (core * core_rows, core_rows),
+            (bases(c)[0], mid_rows),
+            (bases(c)[2], low_rows),
         )[stage]
-        return remote(src.at[c], dst.at[c], rs_send.at[stage, c], rs_recv.at[stage, c], device)
-
-    def gather_copy(stage, c):
-        base, count, device = (
-            (core_base, core_rows, sibling),
-            (core_base + y_base, y_rows, across),
-            (core_base + y_base + x_base, x_rows, partner),
-        )[stage]
-        block = final.at[c, pl.ds(pl.multiple_of(base, count), count)]
+        block = final.at[c, span(base, count)]
+        device = device_of(stage, c)
         return remote(block, block, ag_send.at[stage, c], ag_recv.at[stage, c], device)
 
+    at_all = at_in[...].reshape(nf * tokens, rows)
+
     for c in range(CHUNKS):
-        acc[c] = dot_tn(
-            at_in[...].reshape(nf * tokens, rows),
-            cot[:, :, c * part : (c + 1) * part].reshape(nf * tokens, part),
-        )
-        core_out[c] = acc[c, pl.ds(core_other, core_rows)].astype(BF16)
+        acc[c] = dot_tn(at_all, cot[:, :, c * part : (c + 1) * part].reshape(nf * tokens, part))
+        core_out[c] = acc[c, span((1 - core) * core_rows, core_rows)].astype(BF16)
         reduce_copy(0, c).start()
 
     def reduce_core(c):
+        mid, mid_other, low, low_other = bases(c)
         reduce_copy(0, c).wait_recv()
-        acc[c, pl.ds(core_base, core_rows)] += core_in[c].astype(F32)
-        y_out[c] = acc[c, pl.ds(core_base + y_other, y_rows)].astype(BF16)
+        there = mid_other - core * core_rows
+        y_out[c] = (
+            acc[c, span(mid_other, mid_rows)] + core_in[c, span(there, mid_rows)].astype(F32)
+        ).astype(BF16)
         reduce_copy(1, c).start()
+        here = mid - core * core_rows
+        acc[c, span(mid, mid_rows)] += core_in[c, span(here, mid_rows)].astype(F32)
 
     def reduce_y(c):
+        mid, mid_other, low, low_other = bases(c)
         reduce_copy(1, c).wait_recv()
-        acc[c, pl.ds(core_base + y_base, y_rows)] += y_in[c].astype(F32)
-        x_out[c] = acc[c, pl.ds(core_base + y_base + x_other, x_rows)].astype(BF16)
+        acc[c, span(mid, mid_rows)] += y_in[c].astype(F32)
+        x_out[c] = acc[c, span(low_other, low_rows)].astype(BF16)
         reduce_copy(2, c).start()
 
     def reduce_x(c):
+        low = bases(c)[2]
         reduce_copy(2, c).wait_recv()
-        mine = pl.ds(core_base + y_base + x_base, x_rows)
+        mine = span(low, low_rows)
         final[c, mine] = (acc[c, mine] + x_in[c].astype(F32)).astype(BF16)
         gather_copy(2, c).start()
 
@@ -404,18 +452,13 @@
         gather_copy(1, c).wait()
         gather_copy(0, c).start()
 
+    def wide_copy(c):
+        cols = slice(c * part, (c + 1) * part)
+        return pltpu.make_async_copy(final.at[c], wg_hbm.at[:, cols], wide_sem.at[c])
+
     def gather_core(c):
         gather_copy(0, c).wait()
-        wg_ref[:, c * part : (c + 1) * part] = final[c]
-
-    for c in range(CHUNKS):
-        reduce_core(c)
-
-    visit_peers(nf - 1, nf, take_go)
-
-    for stage in (reduce_y, reduce_x, gather_x, gather_y):
-        for c in range(CHUNKS):
-            stage(c)
+        wide_copy(c).start()
 
     def finish(g):
         cols = pl.ds(pl.multiple_of(g * rows, rows), rows)
@@ -423,13 +466,34 @@
             kv_copy(which, g).wait()
             out[:, cols] = (kv_own[which, g] + kv_in[which, g].astype(F32)).astype(BF16)
 
-    finish(f)
-    visit_peers(1, nf, finish)
+    stores = [
+        pltpu.make_async_copy(src, dst, store_sem.at[i])
+        for i, (src, dst) in enumerate(((qg_ref, qg_hbm), (kg_ref, kg_hbm), (vg_ref, vg_hbm)))
+    ]
+
+    def finish_all():
+        finish(f)
+        visit_peers(1, nf, finish)
+        for store in stores:
+            store.start()
+
+    visit_peers(nf - 1, nf, take_go)
+
+    stages = (reduce_core, reduce_y, reduce_x, gather_x, gather_y, gather_core)
+    for t in range(CHUNKS + len(stages) - 1):
+        for stage in reversed(range(len(stages))):
+            if 0 <= t - stage < CHUNKS:
+                stages[stage](t - stage)
+        if t == CHUNKS:
+            finish_all()
 
     for c in range(CHUNKS):
-        gather_core(c)
+        wide_copy(c).wait()
         for stage in range(3):
             reduce_copy(stage, c).wait_send()
+
+    for store in stores:
+        store.wait()
 
     def drain(j):
         go_copy(j, j).wait_send()
@@ -447,11 +511,36 @@
 
     @pl.when(f + 1 < nf)
     def _():
-        cot_up(f).wait_send()
+        own_up.wait_send()
 
     @pl.when(f > 0)
     def _():
-        cot_down(f).wait_send()
+        own_down.wait_send()
+
+
+def store_kernel(
+    factor, qg, kg, vg, wg, qg_out, kg_out, vg_out, wg_out, narrow, wide, sems, in_sems, out_sems
+):
+    count = wg.shape[0] // STORES
+    blocks = [slice(i * count, (i + 1) * count) for i in range(STORES)]
+    loads = [
+        pltpu.make_async_copy(wg.at[block], narrow.at[block], in_sems.at[i])
+        for i, block in enumerate(blocks)
+    ]
+    copies = [
+        pltpu.make_async_copy(src, dst, sems.at[i])
+        for i, (src, dst) in enumerate(((qg, qg_out), (kg, kg_out), (vg, vg_out)))
+    ]
+    for copy in loads + copies:
+        copy.start()
+    for i, block in enumerate(blocks):
+        loads[i].wait()
+        wide[block, :] = narrow[block, :].astype(F32) * factor
+        copy = pltpu.make_async_copy(wide.at[block], wg_out.at[block], out_sems.at[i])
+        copy.start()
+        copies.append(copy)
+    for copy in copies:
+        copy.wait()
 
 
 def fused_body(nf, queries, key_rows, value_rows, cotangent, out_weight):
@@ -459,7 +548,6 @@
     tokens, heads_width = queries.shape[1:]
     rows, width = out_weight.shape
     part = width // CHUNKS
-    vmem = pl.BlockSpec(memory_space=pltpu.VMEM)
     dma = pltpu.SemaphoreType.DMA
     outs = pl.pallas_call(
         functools.partial(fused_kernel, nf),
@@ -469,8 +557,8 @@
             jax.ShapeDtypeStruct((tokens, heads_width), BF16),
             jax.ShapeDtypeStruct((rows, width), BF16),
         ),
-        in_specs=[vmem] * 5,
-        out_specs=[vmem] * 4,
+        in_specs=[pl.BlockSpec(memory_space=pltpu.HBM)] * 5,
+        out_specs=[pl.BlockSpec(memory_space=pltpu.HBM)] * 4,
         scratch_shapes=[
             pltpu.VMEM((nf, tokens, width), BF16),
             pltpu.VMEM((2, tokens, heads_width), BF16),
@@ -491,10 +579,18 @@
             pltpu.VMEM((CHUNKS, rows // 8, part), BF16),
             pltpu.VMEM((CHUNKS, rows // 8, part), BF16),
             pltpu.VMEM((CHUNKS, rows, part), BF16),
+            pltpu.VMEM((tokens, heads_width), BF16),
+            pltpu.VMEM((rows, width), BF16),
+            pltpu.VMEM((tokens, heads_width), BF16),
+            pltpu.VMEM((tokens, heads_width), BF16),
+            pltpu.VMEM((tokens, heads_width), BF16),
+            dma((5,)),
+            dma((3,)),
+            dma((CHUNKS,)),
             dma((2, nf)),
             dma((nf,)),
-            dma((2,)),
-            dma((2,)),
+            dma((2, nf)),
+            dma((2, nf)),
             dma((nf,)),
             dma((nf,)),
             dma((nf,)),
@@ -507,10 +603,25 @@
             dma((3, CHUNKS)),
         ],
         compiler_params=pltpu.CompilerParams(
-            collective_id=0, has_side_effects=True, vmem_limit_bytes=48 * 1024 * 1024
+            collective_id=0, has_side_effects=True, vmem_limit_bytes=58 * 1024 * 1024
         ),
     )(queries[0], key_rows[0], value_rows[0], cotangent[0], out_weight)
-    return (outs[0][None], outs[1][None], outs[2][None], outs[3].astype(F32) / samples)
+    stored = pl.pallas_call(
+        functools.partial(store_kernel, 1.0 / samples),
+        out_shape=tuple(jax.ShapeDtypeStruct(out.shape, out.dtype) for out in outs[:3])
+        + (jax.ShapeDtypeStruct((rows, width), F32),),
+        in_specs=[pl.BlockSpec(memory_space=pltpu.HBM)] * 4,
+        out_specs=[pl.BlockSpec(memory_space=pltpu.HBM)] * 4,
+        scratch_shapes=[
+            pltpu.VMEM((rows, width), BF16),
+            pltpu.VMEM((rows, width), F32),
+            dma((3,)),
+            dma((STORES,)),
+            dma((STORES,)),
+        ],
+        compiler_params=pltpu.CompilerParams(vmem_limit_bytes=58 * 1024 * 1024),
+    )(*outs)
+    return tuple(out[None] for out in stored[:3]) + (stored[3],)
 
 
 def pick_body(mesh):

time: 105 us -> 163 us (1.55)
  the two profiles are of different devices: /device:TPU:0 before, /device:TPU:25 now
where the time goes in v2:
time: 163 us
  Pallas kernels  163 us (100%)
    pallas_call x1, Pallas kernels, fused_body(): pl.pallas_call(functools.partial(fused_kernel, nf), out_shape=(jax.ShapeD...  114 us
    pallas_call x1, Pallas kernels, fused_body(): pl.pallas_call(functools.partial(store_kernel, 1.0 / samples), out_shape=...  48.9 us

profile of v2, /device:TPU:25, one launch (start us, length us, event | category | flops | bytes accessed | tf_op | source)
XLA Modules:
  0.0 163.3 jit_solution(9491841381984799789)
XLA Ops:
  0.6 113.8 %shard_map.84 = (bf16[128,2048]{1,0:T(8,128)(2,1)}, bf16[128,2048]{1,0:T(8,128)(2,1)}, bf16[128,2048]{1,0:T(8,128)(2,1)}, bf16[512,2048]{1,0:T(8,128)(2,1)}) custom-call(bf16[128,2048]{1,0:T(8,128)(2,1)} %bitcast.7, bf16[128,2048]{1,0:T(8,128)(2,1)} %bitcast.8, bf16[128,2048]{1,0:T(8,128)(2,1)} %bitcast.9, bf16[128,2048]{1,0:T(8,128)(2,1)} %bitcast.10, ...), custom_call_target="tpu_custom_call" | custom-call | tf_op jit(solution)/shard_map/pallas_call | solution.py:552
  114.4 48.9 %shard_map.85 = (bf16[128,2048]{1,0:T(8,128)(2,1)}, bf16[128,2048]{1,0:T(8,128)(2,1)}, bf16[128,2048]{1,0:T(8,128)(2,1)}, f32[512,2048]{1,0:T(8,128)}) custom-call(bf16[128,2048]{1,0:T(8,128)(2,1)} %get-tuple-element.12.qg, bf16[128,2048]{1,0:T(8,128)(2,1)} %get-tuple-element.13.kg, bf16[128,2048]{1,0:T(8,128)(2,1)} %get-tuple-element.14.vg, ...), custom_call_target="tpu_custom_call" | custom-call | tf_op jit(solution)/shard_map/pallas_call | solution.py:609

commit v3 on v2

--- a/solution.py
+++ b/solution.py
@@ -9,7 +9,7 @@
 
 DH = 128
 CHUNKS = 4
-X_FIRST = (3,)
+X_FIRST = (1, 3)
 STORES = 8
 F32 = jnp.float32
 BF16 = jnp.bfloat16
@@ -164,6 +164,7 @@
     kg_ref,
     vg_ref,
     load_sem,
+    pair_sem,
     store_sem,
     wide_sem,
     cot_send,
@@ -210,14 +211,26 @@
             (
                 (c_hbm, cot.at[f]),
                 (w_hbm, w_ref),
-                (k_hbm, keys.at[0]),
-                (v_hbm, vals.at[0]),
                 (q_hbm, q_ref),
             )
         )
     ]
-    for load in loads:
-        load.start()
+
+    def group_at(i):
+        return (f + 1 + i) % nf
+
+    def pair_load(which, i):
+        g = group_at(i)
+        cols = pl.ds(pl.multiple_of(g * rows, rows), rows)
+        src, dst = ((k_hbm, keys), (v_hbm, vals))[which]
+        return pltpu.make_async_copy(src.at[:, cols], dst.at[0, g], pair_sem.at[which, i])
+
+    loads[0].start()
+    for i in range(nf):
+        pair_load(0, i).start()
+        pair_load(1, i).start()
+    loads[1].start()
+    loads[2].start()
 
     barrier = pltpu.get_barrier_semaphore()
     for device in (sibling, across, partner):
@@ -257,37 +270,35 @@
     def wait_into(ref, sem):
         pltpu.make_async_copy(ref, ref, sem).wait()
 
-    own_up = remote(c_hbm, cot.at[f], cot_send.at[0, f], cot_recv.at[f], {"fsdp": f + 1})
-    own_down = remote(c_hbm, cot.at[f], cot_send.at[1, f], cot_recv.at[f], {"fsdp": f - 1})
+    loads[0].wait()
 
     @pl.when(f + 1 < nf)
     def _():
-        own_up.start()
+        cot_up(f).start()
 
     @pl.when(f > 0)
     def _():
-        own_down.start()
+        cot_down(f).start()
 
     def pair_copy(which, i):
-        g = (f + 1 + i) % nf
-        cols = pl.ds(pl.multiple_of(g * rows, rows), rows)
-        src, dst = ((k_hbm, keys), (v_hbm, vals))[which]
+        g = group_at(i)
+        buffer = (keys, vals)[which]
         return remote(
-            src.at[:, cols],
-            dst.at[1, :, cols],
+            buffer.at[0, g],
+            buffer.at[1, g],
             pair_send.at[which, i],
             pair_recv.at[which, i],
             partner,
         )
 
     for i in range(nf):
-        pair_copy(0, i).start()
-        pair_copy(1, i).start()
+        for which in range(2):
+            pair_load(which, i).wait()
+            pair_copy(which, i).start()
 
     def project(j):
         return dot_nt(cot[j], w_ref[...]).astype(BF16)
 
-    loads[0].wait()
     loads[1].wait()
     go_in[f] = project(f)
 
@@ -319,14 +330,15 @@
         go_copy(j, j).start()
 
     def soften(i):
-        g = (f + 1 + i) % nf
+        g = group_at(i)
         base = g * rows
         pair_copy(0, i).wait()
         pair_copy(1, i).wait()
         for t in range(group_heads):
             cols = pl.ds(pl.multiple_of(base + t * DH, DH), DH)
-            kh = keys[:, :, cols].reshape(2 * tokens, DH)
-            vh = vals[:, :, cols].reshape(2 * tokens, DH)
+            inner = slice(t * DH, (t + 1) * DH)
+            kh = keys[:, g, :, inner].reshape(2 * tokens, DH)
+            vh = vals[:, g, :, inner].reshape(2 * tokens, DH)
             scores = dot_nt(q_ref[:, cols], kh) * scale
             highest = jnp.max(scores, axis=1, keepdims=True)
             expanded = jnp.exp(scores - highest)
@@ -345,8 +357,8 @@
         for t in range(group_heads):
             cols = pl.ds(pl.multiple_of(base + t * DH, DH), DH)
             inner = slice(t * DH, (t + 1) * DH)
-            kh = keys[:, :, cols].reshape(2 * tokens, DH)
-            vh = vals[:, :, cols].reshape(2 * tokens, DH)
+            kh = keys[:, g, :, inner].reshape(2 * tokens, DH)
+            vh = vals[:, g, :, inner].reshape(2 * tokens, DH)
             qh = q_ref[:, cols]
             gh = go_in[g, :, inner]
             weights = probs[g * group_heads + t]
@@ -367,13 +379,12 @@
         wait_into(go_in.at[j], go_recv.at[j])
         differentiate(j)
 
-    for load in loads[2:]:
-        load.wait()
-    soften(0)
-    for d in range(1, nf):
-        visit_peers(d, d + 1, take_cot)
+    loads[2].wait()
+    visit_peers(1, nf - 1, take_cot)
+    for d in range(nf):
         soften(d)
     differentiate(f)
+    visit_peers(nf - 1, nf, take_cot)
     visit_peers(1, nf - 1, take_go)
 
     visit_peers(1, nf, lambda j: wait_into(at_in.at[j], at_recv.at[j]))
@@ -477,15 +488,19 @@
         for store in stores:
             store.start()
 
+    for c in range(CHUNKS):
+        reduce_core(c)
+
     visit_peers(nf - 1, nf, take_go)
 
-    stages = (reduce_core, reduce_y, reduce_x, gather_x, gather_y, gather_core)
-    for t in range(CHUNKS + len(stages) - 1):
-        for stage in reversed(range(len(stages))):
-            if 0 <= t - stage < CHUNKS:
-                stages[stage](t - stage)
-        if t == CHUNKS:
-            finish_all()
+    for stage in (reduce_y, reduce_x, gather_x, gather_y):
+        for c in range(CHUNKS):
+            stage(c)
+
+    finish_all()
+
+    for c in range(CHUNKS):
+        gather_core(c)
 
     for c in range(CHUNKS):
         wide_copy(c).wait()
@@ -511,15 +526,29 @@
 
     @pl.when(f + 1 < nf)
     def _():
-        own_up.wait_send()
+        cot_up(f).wait_send()
 
     @pl.when(f > 0)
     def _():
-        own_down.wait_send()
+        cot_down(f).wait_send()
 
 
 def store_kernel(
-    factor, qg, kg, vg, wg, qg_out, kg_out, vg_out, wg_out, narrow, wide, sems, in_sems, out_sems
+    factor,
+    qg,
+    kg,
+    vg,
+    wg,
+    qg_out,
+    kg_out,
+    vg_out,
+    wg_out,
+    held,
+    narrow,
+    wide,
+    sems,
+    in_sems,
+    out_sems,
 ):
     count = wg.shape[0] // STORES
     blocks = [slice(i * count, (i + 1) * count) for i in range(STORES)]
@@ -527,18 +556,24 @@
         pltpu.make_async_copy(wg.at[block], narrow.at[block], in_sems.at[i])
         for i, block in enumerate(blocks)
     ]
+    fills = [
+        pltpu.make_async_copy(src, held.at[i], sems.at[0, i]) for i, src in enumerate((qg, kg, vg))
+    ]
     copies = [
-        pltpu.make_async_copy(src, dst, sems.at[i])
-        for i, (src, dst) in enumerate(((qg, qg_out), (kg, kg_out), (vg, vg_out)))
+        pltpu.make_async_copy(held.at[i], dst, sems.at[1, i])
+        for i, dst in enumerate((qg_out, kg_out, vg_out))
     ]
-    for copy in loads + copies:
+    for copy in loads + fills:
         copy.start()
     for i, block in enumerate(blocks):
         loads[i].wait()
         wide[block, :] = narrow[block, :].astype(F32) * factor
-        copy = pltpu.make_async_copy(wide.at[block], wg_out.at[block], out_sems.at[i])
+        pltpu.make_async_copy(wide.at[block], wg_out.at[block], out_sems.at[i]).start()
+    for fill, copy in zip(fills, copies):
+        fill.wait()
         copy.start()
-        copies.append(copy)
+    for i, block in enumerate(blocks):
+        pltpu.make_async_copy(wide.at[block], wg_out.at[block], out_sems.at[i]).wait()
     for copy in copies:
         copy.wait()
 
@@ -561,8 +596,8 @@
         out_specs=[pl.BlockSpec(memory_space=pltpu.HBM)] * 4,
         scratch_shapes=[
             pltpu.VMEM((nf, tokens, width), BF16),
-            pltpu.VMEM((2, tokens, heads_width), BF16),
-            pltpu.VMEM((2, tokens, heads_width), BF16),
+            pltpu.VMEM((2, nf, tokens, rows), BF16),
+            pltpu.VMEM((2, nf, tokens, rows), BF16),
             pltpu.VMEM((nf, tokens, rows), BF16),
             pltpu.VMEM((nf, tokens, rows), BF16),
             pltpu.VMEM((nf, tokens, rows), BF16),
@@ -584,7 +619,8 @@
             pltpu.VMEM((tokens, heads_width), BF16),
             pltpu.VMEM((tokens, heads_width), BF16),
             pltpu.VMEM((tokens, heads_width), BF16),
-            dma((5,)),
+            dma((3,)),
+            dma((2, nf)),
             dma((3,)),
             dma((CHUNKS,)),
             dma((2, nf)),
@@ -613,9 +649,10 @@
         in_specs=[pl.BlockSpec(memory_space=pltpu.HBM)] * 4,
         out_specs=[pl.BlockSpec(memory_space=pltpu.HBM)] * 4,
         scratch_shapes=[
+            pltpu.VMEM((3, tokens, heads_width), BF16),
             pltpu.VMEM((rows, width), BF16),
             pltpu.VMEM((rows, width), F32),
-            dma((3,)),
+            dma((2, 3)),
             dma((STORES,)),
             dma((STORES,)),
         ],

time: 163 us -> 96.8 us (0.59)
  the two profiles are of different devices: /device:TPU:25 before, /device:TPU:0 now
where the time goes in v3:
time: 96.8 us; the launch traced here: 96.7 us
  Pallas kernels  96.1 us (99%)
    pallas_call x1, Pallas kernels, fused_body(): pl.pallas_call(functools.partial(fused_kernel, nf), out_shape=(jax.ShapeD...  92.4 us
    pallas_call x1, Pallas kernels, fused_body(): pl.pallas_call(functools.partial(store_kernel, 1.0 / samples), out_shape=...  3.67 us

profile of v3, /device:TPU:0, one launch (start us, length us, event | category | flops | bytes accessed | tf_op | source)
XLA Modules:
  0.0 96.7 jit_solution(2434132157059402693)
XLA Ops:
  0.6 92.4 %shard_map.84 = (bf16[128,2048]{1,0:T(8,128)(2,1)}, bf16[128,2048]{1,0:T(8,128)(2,1)}, bf16[128,2048]{1,0:T(8,128)(2,1)}, bf16[512,2048]{1,0:T(8,128)(2,1)}) custom-call(bf16[128,2048]{1,0:T(8,128)(2,1)} %bitcast.7, bf16[128,2048]{1,0:T(8,128)(2,1)} %bitcast.8, bf16[128,2048]{1,0:T(8,128)(2,1)} %bitcast.9, bf16[128,2048]{1,0:T(8,128)(2,1)} %bitcast.10, ...), custom_call_target="tpu_custom_call" | custom-call | tf_op jit(solution)/shard_map/pallas_call | solution.py:587
  93.0 3.7 %shard_map.85 = (bf16[128,2048]{1,0:T(8,128)(2,1)}, bf16[128,2048]{1,0:T(8,128)(2,1)}, bf16[128,2048]{1,0:T(8,128)(2,1)}, f32[512,2048]{1,0:T(8,128)}) custom-call(bf16[128,2048]{1,0:T(8,128)(2,1)} %get-tuple-element.12.qg, bf16[128,2048]{1,0:T(8,128)(2,1)} %get-tuple-element.13.kg, bf16[128,2048]{1,0:T(8,128)(2,1)} %get-tuple-element.14.vg, ...), custom_call_target="tpu_custom_call" | custom-call | tf_op jit(solution)/shard_map/pallas_call | solution.py:645
